TPU v7x, 128 devices: a whole 4x4x4 slice. The times are simulated.
128 devices in a mesh: prow: 16 (over z, y), pcol: 4 (over x), layer: 2 (over core).
Axes of the slice: x: 4, y: 4, z: 4, core: 2. Of those that a mesh axis runs over, the one named last changes fastest.
Arguments:
- rhs_sub: float32 [2, 2, 16, 256, 256], P('layer', None, 'prow'), may hold values from -6 to 6
- l_blocks: bfloat16 [2, 1, 16, 16, 256, 256], P('layer', None, 'prow', 'pcol'), may hold values from -0.09375 to 0.09375
- u_blocks: bfloat16 [2, 1, 16, 16, 256, 256], P('layer', None, 'prow', 'pcol'), may hold values from -0.09375 to 0.09375
- l_pattern: int32 [2, 1, 16, 16], P('layer', None, 'prow', 'pcol'), may hold values 0 or 1
- u_pattern: int32 [2, 1, 16, 16], P('layer', None, 'prow', 'pcol'), may hold values 0 or 1
- l_diag_inv: bfloat16 [2, 2, 16, 256, 256], P('layer', None, 'prow'), may hold values from -1.4 to 1.4, as said below
- u_diag_inv: bfloat16 [2, 2, 16, 256, 256], P('layer', None, 'prow'), may hold values from -1.4 to 1.4, as said below
- sub_sizes: int32 [2, 2, 16], P('layer', None, 'prow'), may hold values from 64 to 256, as said below
- rhs_root: float32 [4, 256, 256], P('pcol'), may hold values from -6 to 6
- root_l: bfloat16 [4, 4, 256, 256], P('pcol', None, None, 'prow'), may hold values from -0.1875 to 0.1875
- root_u: bfloat16 [4, 4, 256, 256], P('pcol', None, None, 'prow'), may hold values from -0.1875 to 0.1875
- root_l_sub: bfloat16 [2, 4, 16, 256, 256], P('layer', 'pcol', 'prow'), may hold values from -0.0625 to 0.0625
- root_u_sub: bfloat16 [2, 16, 4, 256, 256], P('layer', 'prow', 'pcol'), may hold values from -0.1875 to 0.1875
- root_l_diag_inv: bfloat16 [4, 256, 256], replicated, may hold values from -1.4 to 1.4, as said below
- root_u_diag_inv: bfloat16 [4, 256, 256], replicated, may hold values from -1.4 to 1.4, as said below
- root_sizes: int32 [4], replicated, may hold values from 64 to 256, as said below
Outputs:
- solution_sub: float32 [2, 2, 16, 256, 256], P('layer', None, 'prow')
- solution_root: float32 [4, 256, 256], P('pcol')
Inputs may be any that keep to these rules, and one draw needn't show every extreme that they name: `sub_sizes`: the used order of each subtree supernode; some supernode of every draw uses all 256. `root_sizes`: the used order of each root supernode; some supernode of every draw uses all 256. `l_diag_inv`: the inverse of a diagonal block of the lower factor. `u_diag_inv`: the inverse of a diagonal block of the upper factor. `root_l_diag_inv`: the inverse of a diagonal block of the lower factor. `root_u_diag_inv`: the inverse of a diagonal block of the upper factor.
All inputs are finite; a program needn't handle non-finite values. No bound on the sum of `l_pattern` or of `u_pattern` on one device may be relied on, other than what follows from the above.
Results may differ from a plain program's by a relative error of at most 0.0075.
Values may be sent and summed in bfloat16 or wider, within the bound.
A program may use at most 64 MiB of HBM per device.

v0:
```python
import jax
import jax.numpy as jnp
from jax import lax
from jax.sharding import PartitionSpec as P

highest = lax.Precision.HIGHEST


def from_root(array, axis, root):
    mine = lax.axis_index(axis) == root
    return lax.psum(jnp.where(mine, array, jnp.zeros_like(array)), axis)


def from_partner(block, axis, apart):
    count = lax.axis_size(axis)
    route = []
    for low in range(count):
        high = low | 1 << apart
        if high != low and high < count:
            route += [(low, high), (high, low)]
    return lax.ppermute(block, axis, route)


def masked_solve(inverse, right_side, used_sizes):
    used_mask = (
        jnp.arange(inverse.shape[-1], dtype=jnp.int32)[None, :] < used_sizes[:, None]
    ).astype(jnp.float32)
    solved = jnp.einsum("nab,nbr->nar", inverse.astype(jnp.float32), right_side, precision=highest)
    return solved * used_mask[:, :, None]


def couple_local(blocks, pattern, columns):
    pattern_bf = pattern.astype(jnp.bfloat16)[:, :, None, None]
    masked_cols = columns[None] * pattern_bf
    return jnp.einsum("nkab,nkbr->nar", blocks, masked_cols, preferred_element_type=jnp.float32)


def couple_dense(blocks, columns):
    return jnp.einsum("nkab,kbr->nar", blocks, columns, preferred_element_type=jnp.float32)


def own_cols(gathered, col_width):
    return lax.dynamic_slice_in_dim(gathered, lax.axis_index("pcol") * col_width, col_width, 0)


def level_step(right_side, partial_value, inverse, used_sizes, spread_out):
    if partial_value is not None:
        right_side = right_side - lax.psum(partial_value, "pcol")
    solved = masked_solve(inverse, right_side, used_sizes)
    narrow = solved.astype(jnp.bfloat16)
    if spread_out:
        return (solved, lax.all_gather(narrow, "prow", axis=0, tiled=True))
    return (solved, narrow)


def chain_solve(right_own, coupling, blocks, inverses, used_sizes, backward):
    row_count = right_own.shape[0]
    total_count = inverses.shape[0]
    slice_width = blocks.shape[3]
    order_b = right_own.shape[1]
    my_row = lax.axis_index("prow")
    my_column = lax.axis_index("pcol")
    portions = 1
    half_width = right_own.shape[2] // portions
    zero_index = jnp.int32(0)

    def chain_turn(counter, carried):
        solved_all, owned = carried
        position = total_count - 1 - counter if backward else counter
        position = jnp.asarray(position, jnp.int32)
        owner_col = position // row_count
        slot_index = position % row_count
        is_owner = my_column == owner_col
        row_blocks = lax.dynamic_index_in_dim(blocks, slot_index, 0, keepdims=False)
        row_right = lax.dynamic_index_in_dim(right_own, slot_index, 0, keepdims=False)
        row_coupling = lax.dynamic_index_in_dim(coupling, slot_index, 0, keepdims=False)
        inverse = lax.dynamic_slice_in_dim(inverses, position, 1, 0)
        used_size = lax.dynamic_slice_in_dim(used_sizes, position, 1, 0)
        offset = jnp.int32(0)
        columns = lax.dynamic_slice(
            solved_all,
            (zero_index, my_row * slice_width, offset),
            (total_count, slice_width, half_width),
        )
        partial_term = jnp.einsum(
            "uab,ubr->ar", row_blocks, columns, preferred_element_type=jnp.float32
        )
        baseline = row_right - row_coupling
        right_side = baseline - lax.psum(partial_term, "prow")
        solved = masked_solve(inverse, right_side[None], used_size)[0]
        narrow = from_root(solved.astype(jnp.bfloat16), "pcol", owner_col)
        solved_all = lax.dynamic_update_slice(
            solved_all, narrow[None], (position, zero_index, offset)
        )
        values = [solved]
        row_old = lax.dynamic_index_in_dim(owned, slot_index, 0, keepdims=False)
        row_new = jnp.where(is_owner, jnp.concatenate(values, axis=1), row_old)
        owned = lax.dynamic_update_index_in_dim(owned, row_new, slot_index, 0)
        return (solved_all, owned)

    initial = (
        jnp.zeros((total_count, order_b, right_own.shape[2]), jnp.bfloat16),
        jnp.zeros_like(right_own),
    )
    solved_all, owned = lax.fori_loop(0, total_count, chain_turn, initial)
    return (owned, solved_all)


def local(
    rhs_sub,
    l_blocks,
    u_blocks,
    l_pattern,
    u_pattern,
    l_diag_inv,
    u_diag_inv,
    sub_sizes,
    rhs_root,
    root_l,
    root_u,
    root_l_sub,
    root_u_sub,
    root_l_diag_inv,
    root_u_diag_inv,
    root_sizes,
):
    levels = rhs_sub.shape[1]
    top_level = levels - 1
    forward = []
    solved, spread = level_step(
        rhs_sub[0, 0], None, l_diag_inv[0, 0], sub_sizes[0, 0], top_level > 0
    )
    forward.append(solved)
    tree_level = 1
    blocks = l_blocks[0, tree_level - 1]
    partial_value = couple_local(
        blocks, l_pattern[0, tree_level - 1], own_cols(spread, blocks.shape[1])
    )
    solved, spread = level_step(
        rhs_sub[0, tree_level],
        partial_value,
        l_diag_inv[0, tree_level],
        sub_sizes[0, tree_level],
        tree_level < top_level,
    )
    forward.append(solved)
    upward = couple_dense(root_l_sub[0], spread)
    upward = lax.psum(upward, "prow")
    upward = upward + from_partner(upward, "layer", 0)
    root_y, solved_y = chain_solve(rhs_root, upward, root_l, root_l_diag_inv, root_sizes, False)
    root_x, solved_x = chain_solve(
        root_y, jnp.zeros_like(rhs_root), root_u, root_u_diag_inv, root_sizes, True
    )
    partial_value = couple_dense(root_u_sub[0], own_cols(solved_x, root_u_sub.shape[2]))
    solved, spread = level_step(
        forward[top_level], partial_value, u_diag_inv[0, top_level], sub_sizes[0, top_level], True
    )
    backward = [solved]
    tree_level = 0
    blocks = u_blocks[0, tree_level]
    partial_value = couple_local(
        blocks, u_pattern[0, tree_level], own_cols(spread, blocks.shape[1])
    )
    solved, spread = level_step(
        forward[tree_level],
        partial_value,
        u_diag_inv[0, tree_level],
        sub_sizes[0, tree_level],
        tree_level > 0,
    )
    backward.insert(0, solved)
    return (jnp.stack(backward, 0)[None], root_x)


def solution(mesh):
    in_specs = (
        P("layer", None, "prow", None, None),
        P("layer", None, "prow", "pcol", None, None),
        P("layer", None, "prow", "pcol", None, None),
        P("layer", None, "prow", "pcol"),
        P("layer", None, "prow", "pcol"),
        P("layer", None, "prow", None, None),
        P("layer", None, "prow", None, None),
        P("layer", None, "prow"),
        P("pcol", None, None),
        P("pcol", None, None, "prow"),
        P("pcol", None, None, "prow"),
        P("layer", "pcol", "prow", None, None),
        P("layer", "prow", "pcol", None, None),
        P(),
        P(),
        P(),
    )
    out_specs = (P("layer", None, "prow", None, None), P("pcol", None, None))
    return jax.shard_map(local, mesh=mesh, in_specs=in_specs, out_specs=out_specs, check_vma=False)
```

profile of v0, /device:TPU:0, one launch (start us, length us, event | category | flops | bytes accessed | tf_op | source)
XLA Modules:
  0.0 1412.1 jit_solution(8592503924905513009)
XLA Ops:
  11.9 47.2 %all-gather.5.cloned.1.call-done = bf16[4096,256]{1,0:T(8,128)(2,1)} async-done(((bf16[256,256]{1,0:T(8,128)(2,1)}), bf16[4096,256]{1,0:T(8,128)(2,1)}) %all-gather.5.cloned.1.call-update) | async-done | bytes 2097168 | tf_op jit(solution)/shard_map/all_gather | solution.py:52
  62.5 40.4 %all-reduce.9.cloned.1.call-done = f32[1,256,256]{1,2,0:T(8,128)} async-done(((f32[1,256,256]{1,2,0:T(8,128)}), f32[1,256,256]{1,2,0:T(8,128)}) %all-reduce.9.cloned.1.call-update) | async-done | bytes 262160 | tf_op jit(solution)/shard_map/psum | solution.py:48
  105.1 86.8 %all-reduce.11.cloned.1.call-done = f32[1,256,256]{1,2,0:T(8,128)} async-done(((f32[1,256,256]{1,2,0:T(8,128)}), f32[1,256,256]{1,2,0:T(8,128)}) %all-reduce.11.cloned.1.call-update) | async-done | bytes 262160 | tf_op jit(solution)/shard_map/psum | solution.py:148
  194.9 532.8 %while.36 = (s32[]{:T(128)}, bf16[4,256,256]{2,1,0:T(8,128)(2,1)S(1)}, f32[1,256,256]{2,1,0:T(8,128)S(1)}, bf16[4,256,256]{2,1,0:T(8,128)(2,1)}, s32[]{:T(128)},...) while((s32[]{:T(128)}, ...), condition=%wide.region_5.6_spmd.clone, body=%wide.region_2.5_spmd.clone.sunk | while | flops 210240000 | bytes 4524335 | solution.py:105
  197.3 85.5 %all-reduce.17.cloned.1.call-done = f32[256,256]{1,0:T(8,128)} async-done(((f32[256,256]{1,0:T(8,128)}), f32[256,256]{1,0:T(8,128)}) %all-reduce.17.cloned.1.call-update) | async-done | bytes 262160 | tf_op jit(solution)/shard_map/while/body/eval_jaxpr/psum | solution.py:89
  284.9 41.1 %all-reduce.19.cloned.1.call-done = bf16[1,256,256]{2,1,0:T(8,128)(2,1)} async-done(((bf16[1,256,256]{2,1,0:T(8,128)(2,1)}), bf16[1,256,256]{2,1,0:T(8,128)(2,1)}) %all-reduce.19.cloned.1.call-update) | async-done | bytes 131088 | tf_op jit(solution)/shard_map/while/body/eval_jaxpr/psum | solution.py:11
  329.4 86.8 %all-reduce.17.cloned.1.call-done = f32[256,256]{1,0:T(8,128)} async-done(((f32[256,256]{1,0:T(8,128)}), f32[256,256]{1,0:T(8,128)}) %all-reduce.17.cloned.1.call-update) | async-done | bytes 262160 | tf_op jit(solution)/shard_map/while/body/eval_jaxpr/psum | solution.py:89
  418.2 41.3 %all-reduce.19.cloned.1.call-done = bf16[1,256,256]{2,1,0:T(8,128)(2,1)} async-done(((bf16[1,256,256]{2,1,0:T(8,128)(2,1)}), bf16[1,256,256]{2,1,0:T(8,128)(2,1)}) %all-reduce.19.cloned.1.call-update) | async-done | bytes 131088 | tf_op jit(solution)/shard_map/while/body/eval_jaxpr/psum | solution.py:11
  462.8 87.1 %all-reduce.17.cloned.1.call-done = f32[256,256]{1,0:T(8,128)} async-done(((f32[256,256]{1,0:T(8,128)}), f32[256,256]{1,0:T(8,128)}) %all-reduce.17.cloned.1.call-update) | async-done | bytes 262160 | tf_op jit(solution)/shard_map/while/body/eval_jaxpr/psum | solution.py:89
  552.0 41.3 %all-reduce.19.cloned.1.call-done = bf16[1,256,256]{2,1,0:T(8,128)(2,1)} async-done(((bf16[1,256,256]{2,1,0:T(8,128)(2,1)}), bf16[1,256,256]{2,1,0:T(8,128)(2,1)}) %all-reduce.19.cloned.1.call-update) | async-done | bytes 131088 | tf_op jit(solution)/shard_map/while/body/eval_jaxpr/psum | solution.py:11
  596.6 86.8 %all-reduce.17.cloned.1.call-done = f32[256,256]{1,0:T(8,128)} async-done(((f32[256,256]{1,0:T(8,128)}), f32[256,256]{1,0:T(8,128)}) %all-reduce.17.cloned.1.call-update) | async-done | bytes 262160 | tf_op jit(solution)/shard_map/while/body/eval_jaxpr/psum | solution.py:89
  685.5 41.3 %all-reduce.19.cloned.1.call-done = bf16[1,256,256]{2,1,0:T(8,128)(2,1)} async-done(((bf16[1,256,256]{2,1,0:T(8,128)(2,1)}), bf16[1,256,256]{2,1,0:T(8,128)(2,1)}) %all-reduce.19.cloned.1.call-update) | async-done | bytes 131088 | tf_op jit(solution)/shard_map/while/body/eval_jaxpr/psum | solution.py:11
  727.8 533.6 %while.37 = (s32[]{:T(128)}, bf16[4,256,256]{2,1,0:T(8,128)(2,1)S(1)}, f32[1,256,256]{2,1,0:T(8,128)S(1)}, bf16[4,256,256]{2,1,0:T(8,128)(2,1)}, f32[1,256,256]{...) while((s32[]{:T(128)}, ...), condition=%wide.region_9.10_spmd.clone, body=%wide.region_6.9_spmd.clone.sunk | while | flops 210240000 | bytes 4524389 | solution.py:105
  730.2 86.8 %all-reduce.21.cloned.1.call-done = f32[256,256]{1,0:T(8,128)} async-done(((f32[256,256]{1,0:T(8,128)}), f32[256,256]{1,0:T(8,128)}) %all-reduce.21.cloned.1.call-update) | async-done | bytes 262160 | tf_op jit(solution)/shard_map/while/body/eval_jaxpr/psum | solution.py:89
  819.1 41.3 %all-reduce.23.cloned.1.call-done = bf16[1,256,256]{2,1,0:T(8,128)(2,1)} async-done(((bf16[1,256,256]{2,1,0:T(8,128)(2,1)}), bf16[1,256,256]{2,1,0:T(8,128)(2,1)}) %all-reduce.23.cloned.1.call-update) | async-done | bytes 131088 | tf_op jit(solution)/shard_map/while/body/eval_jaxpr/psum | solution.py:11
  863.7 86.8 %all-reduce.21.cloned.1.call-done = f32[256,256]{1,0:T(8,128)} async-done(((f32[256,256]{1,0:T(8,128)}), f32[256,256]{1,0:T(8,128)}) %all-reduce.21.cloned.1.call-update) | async-done | bytes 262160 | tf_op jit(solution)/shard_map/while/body/eval_jaxpr/psum | solution.py:89
  952.5 41.1 %all-reduce.23.cloned.1.call-done = bf16[1,256,256]{2,1,0:T(8,128)(2,1)} async-done(((bf16[1,256,256]{2,1,0:T(8,128)(2,1)}), bf16[1,256,256]{2,1,0:T(8,128)(2,1)}) %all-reduce.23.cloned.1.call-update) | async-done | bytes 131088 | tf_op jit(solution)/shard_map/while/body/eval_jaxpr/psum | solution.py:11
  997.0 86.8 %all-reduce.21.cloned.1.call-done = f32[256,256]{1,0:T(8,128)} async-done(((f32[256,256]{1,0:T(8,128)}), f32[256,256]{1,0:T(8,128)}) %all-reduce.21.cloned.1.call-update) | async-done | bytes 262160 | tf_op jit(solution)/shard_map/while/body/eval_jaxpr/psum | solution.py:89
  1085.8 41.1 %all-reduce.23.cloned.1.call-done = bf16[1,256,256]{2,1,0:T(8,128)(2,1)} async-done(((bf16[1,256,256]{2,1,0:T(8,128)(2,1)}), bf16[1,256,256]{2,1,0:T(8,128)(2,1)}) %all-reduce.23.cloned.1.call-update) | async-done | bytes 131088 | tf_op jit(solution)/shard_map/while/body/eval_jaxpr/psum | solution.py:11
  1130.3 86.8 %all-reduce.21.cloned.1.call-done = f32[256,256]{1,0:T(8,128)} async-done(((f32[256,256]{1,0:T(8,128)}), f32[256,256]{1,0:T(8,128)}) %all-reduce.21.cloned.1.call-update) | async-done | bytes 262160 | tf_op jit(solution)/shard_map/while/body/eval_jaxpr/psum | solution.py:89
  1219.2 41.3 %all-reduce.23.cloned.1.call-done = bf16[1,256,256]{2,1,0:T(8,128)(2,1)} async-done(((bf16[1,256,256]{2,1,0:T(8,128)(2,1)}), bf16[1,256,256]{2,1,0:T(8,128)(2,1)}) %all-reduce.23.cloned.1.call-update) | async-done | bytes 131088 | tf_op jit(solution)/shard_map/while/body/eval_jaxpr/psum | solution.py:11
  1262.4 44.5 %all-reduce.13.cloned.1.call-done = f32[1,256,256]{1,2,0:T(8,128)} async-done(((f32[1,256,256]{1,2,0:T(8,128)}), f32[1,256,256]{1,2,0:T(8,128)}) %all-reduce.13.cloned.1.call-update) | async-done | bytes 262160 | tf_op jit(solution)/shard_map/psum | solution.py:48
  1309.0 49.2 %all-gather.7.cloned.1.call-done = bf16[4096,256]{0,1:T(8,128)(2,1)} async-done(((bf16[256,256]{0,1:T(8,128)(2,1)}), bf16[4096,256]{0,1:T(8,128)(2,1)}) %all-gather.7.cloned.1.call-update) | async-done | bytes 2097168 | tf_op jit(solution)/shard_map/all_gather | solution.py:52
  1361.9 41.0 %all-reduce.15.cloned.1.call-done = f32[1,256,256]{2,1,0:T(8,128)} async-done(((f32[1,256,256]{2,1,0:T(8,128)}), f32[1,256,256]{2,1,0:T(8,128)}) %all-reduce.15.cloned.1.call-update) | async-done | bytes 262160 | tf_op jit(solution)/shard_map/psum | solution.py:48
  (147 shorter events, 65.0 us)
Async XLA Ops:
  7.2 51.9 %all-gather.5.cloned.1.call-start = ((), (), s32[]{:S(2)}) async-start(), calls=%async_computation.4 | async-start | bytes 2228224 | tf_op jit(solution)/shard_map/all_gather | solution.py:52
  11.2 91.7 %all-reduce.9.cloned.1.call-start = ((), (), s32[]{:S(2)}) async-start(), calls=%async_computation | async-start | bytes 524288 | tf_op jit(solution)/shard_map/psum | solution.py:48
  61.6 130.3 %all-reduce.11.cloned.1.call-start = ((), (), s32[]{:S(2)}) async-start(), calls=%async_computation.1 | async-start | bytes 524288 | tf_op jit(solution)/shard_map/psum | solution.py:148
  191.9 1.7 collective-permute-start
  194.9 87.9 %all-reduce.17.cloned.1.call-start = ((), (), s32[]{:S(2)}) async-start(), calls=%async_computation.6 | async-start | bytes 524288 | tf_op jit(solution)/shard_map/while/body/eval_jaxpr/psum | solution.py:89
  195.9 130.1 %all-reduce.19.cloned.1.call-start = ((), (), s32[]{:S(2)}) async-start(), calls=%async_computation.7 | async-start | bytes 262144 | tf_op jit(solution)/shard_map/while/body/eval_jaxpr/psum | solution.py:11
  327.0 89.2 %all-reduce.17.cloned.1.call-start = ((), (), s32[]{:S(2)}) async-start(), calls=%async_computation.6 | async-start | bytes 524288 | tf_op jit(solution)/shard_map/while/body/eval_jaxpr/psum | solution.py:89
  328.0 131.5 %all-reduce.19.cloned.1.call-start = ((), (), s32[]{:S(2)}) async-start(), calls=%async_computation.7 | async-start | bytes 262144 | tf_op jit(solution)/shard_map/while/body/eval_jaxpr/psum | solution.py:11
  460.4 89.5 %all-reduce.17.cloned.1.call-start = ((), (), s32[]{:S(2)}) async-start(), calls=%async_computation.6 | async-start | bytes 524288 | tf_op jit(solution)/shard_map/while/body/eval_jaxpr/psum | solution.py:89
  461.4 131.8 %all-reduce.19.cloned.1.call-start = ((), (), s32[]{:S(2)}) async-start(), calls=%async_computation.7 | async-start | bytes 262144 | tf_op jit(solution)/shard_map/while/body/eval_jaxpr/psum | solution.py:11
  594.2 89.2 %all-reduce.17.cloned.1.call-start = ((), (), s32[]{:S(2)}) async-start(), calls=%async_computation.6 | async-start | bytes 524288 | tf_op jit(solution)/shard_map/while/body/eval_jaxpr/psum | solution.py:89
  595.2 131.5 %all-reduce.19.cloned.1.call-start = ((), (), s32[]{:S(2)}) async-start(), calls=%async_computation.7 | async-start | bytes 262144 | tf_op jit(solution)/shard_map/while/body/eval_jaxpr/psum | solution.py:11
  727.8 581.2 %copy-start.11 = (s32[1,1,1,4]{3,2,1,0:T(1,128)S(1)}, s32[1,1,1,4]{3,2,1,0:T(1,128)}, u32[]{:S(2)}) copy-start(s32[1,1,1,4]{3,2,1,0:T(1,128)} %param.24) | copy-start | bytes 52
  727.8 89.2 %all-reduce.21.cloned.1.call-start = ((), (), s32[]{:S(2)}) async-start(), calls=%async_computation.8 | async-start | bytes 524288 | tf_op jit(solution)/shard_map/while/body/eval_jaxpr/psum | solution.py:89
  728.8 131.5 %all-reduce.23.cloned.1.call-start = ((), (), s32[]{:S(2)}) async-start(), calls=%async_computation.9 | async-start | bytes 262144 | tf_op jit(solution)/shard_map/while/body/eval_jaxpr/psum | solution.py:11
  861.3 89.2 %all-reduce.21.cloned.1.call-start = ((), (), s32[]{:S(2)}) async-start(), calls=%async_computation.8 | async-start | bytes 524288 | tf_op jit(solution)/shard_map/while/body/eval_jaxpr/psum | solution.py:89
  862.3 131.4 %all-reduce.23.cloned.1.call-start = ((), (), s32[]{:S(2)}) async-start(), calls=%async_computation.9 | async-start | bytes 262144 | tf_op jit(solution)/shard_map/while/body/eval_jaxpr/psum | solution.py:11
  994.6 89.2 %all-reduce.21.cloned.1.call-start = ((), (), s32[]{:S(2)}) async-start(), calls=%async_computation.8 | async-start | bytes 524288 | tf_op jit(solution)/shard_map/while/body/eval_jaxpr/psum | solution.py:89
  995.6 131.4 %all-reduce.23.cloned.1.call-start = ((), (), s32[]{:S(2)}) async-start(), calls=%async_computation.9 | async-start | bytes 262144 | tf_op jit(solution)/shard_map/while/body/eval_jaxpr/psum | solution.py:11
  1127.9 89.2 %all-reduce.21.cloned.1.call-start = ((), (), s32[]{:S(2)}) async-start(), calls=%async_computation.8 | async-start | bytes 524288 | tf_op jit(solution)/shard_map/while/body/eval_jaxpr/psum | solution.py:89
  1128.9 131.5 %all-reduce.23.cloned.1.call-start = ((), (), s32[]{:S(2)}) async-start(), calls=%async_computation.9 | async-start | bytes 262144 | tf_op jit(solution)/shard_map/while/body/eval_jaxpr/psum | solution.py:11
  1261.4 45.5 %all-reduce.13.cloned.1.call-start = ((), (), s32[]{:S(2)}) async-start(), calls=%async_computation.2 | async-start | bytes 524288 | tf_op jit(solution)/shard_map/psum | solution.py:48
  1262.4 95.8 %all-gather.7.cloned.1.call-start = ((), (), s32[]{:S(2)}) async-start(), calls=%async_computation.5 | async-start | bytes 2228224 | tf_op jit(solution)/shard_map/all_gather | solution.py:52
  1308.9 94.0 %all-reduce.15.cloned.1.call-start = ((), (), s32[]{:S(2)}) async-start(), calls=%async_computation.3 | async-start | bytes 524288 | tf_op jit(solution)/shard_map/psum | solution.py:48
  (12 other events, 2286.1 us)
Sparse Core Ops, SparseCore 0:
  11.3 47.7 all-gather.4
  62.0 40.8 all-reduce.8
  107.0 84.9 all-reduce.10
  199.2 83.6 all-reduce.16
  285.7 40.3 all-reduce.18
  331.3 84.8 all-reduce.16
  419.1 40.3 all-reduce.18
  465.0 84.8 all-reduce.16
  552.9 40.3 all-reduce.18
  598.5 84.8 all-reduce.16
  686.4 40.3 all-reduce.18
  732.1 84.8 all-reduce.20
  820.0 40.3 all-reduce.22
  865.5 84.8 all-reduce.20
  953.3 40.3 all-reduce.22
  998.9 84.8 all-reduce.20
  1086.6 40.3 all-reduce.22
  1132.2 84.8 all-reduce.20
  1220.1 40.3 all-reduce.22
  1264.8 42.0 all-reduce.12
  1309.8 48.2 all-gather.6
  1362.0 40.8 all-reduce.14
where the time goes:
time: 1410 us
  waiting for transfers between devices  1330 us (94%)
  matrix products  29.1 us (2%)
  local copies, waits for them, and re-layouts  19.2 us (1%)
  between operations  14.4 us (1%)
    psum x8, waiting for transfers between devices, chain_turn(): right_side = baseline - lax.psum(partial_term, 'prow')  693 us
    psum x8, waiting for transfers between devices, from_root(): return lax.psum(jnp.where(mine, array, jnp.zeros_like(array)), axis)  330 us
    psum x3, waiting for transfers between devices, level_step(): right_side = right_side - lax.psum(partial_value, 'pcol')  126 us
    all_gather x2, waiting for transfers between devices, level_step(): return (solved, lax.all_gather(narrow, 'prow', axis=0, tiled=True))  96.4 us
    psum x1, waiting for transfers between devices, local(): upward = lax.psum(upward, 'prow')  86.8 us
  transfers between devices with their start and end apart: 23, of which 23 were waited for; matrix products, arithmetic and copies ran while one was open for 1% of the time, Pallas kernels for 0%

commit v1 on v0

v1 whole, which is shorter than its diff:
```python
import functools

import jax
import jax.numpy as jnp
from jax import lax
from jax.experimental import pallas as pl
from jax.experimental.pallas import tpu as pltpu
from jax.sharding import PartitionSpec as P

MESH = pl.DeviceIdType.MESH
F32 = jnp.float32
BF = jnp.bfloat16
B = 256
W = 64

PLANE = sorted(
    [(dz, dy, dc) for dz in range(4) for dy in range(4) for dc in range(2) if (dz, dy, dc) != (0, 0, 0)],
    key=lambda o: (-(min(o[0], 4 - o[0]) + min(o[1], 4 - o[1])), o[2]),
)
SAME = [o for o in PLANE if o[2] == 0]
FAR = (2, 1, 3)

COUNT = 0


def take(n):
    global COUNT
    first = COUNT
    COUNT += n
    return first


S_A = take(12)
S_B = take(12)
S_RL = take(4)
S_RU = take(4)
S_U = take(4)
S_RX = take(4)
S_RR = take(4)
S_P = take(4)
S_RP = take(len(SAME))
S_RC = take(1)
S_RS = take(len(PLANE))
S_AG = take(len(PLANE))
S_X = take(len(SAME))
S_XG = take(4)
S_SR = take(4)
S_V = take(4)


def nt(a, b):
    return lax.dot_general(a, b, (((1,), (1,)), ((), ())), preferred_element_type=F32)


def nn(a, b):
    return lax.dot_general(a, b, (((1,), (0,)), ((), ())), preferred_element_type=F32)


def solve(right, inverse, twice):
    high = right.astype(BF)
    out = nt(high, inverse)
    if twice:
        out = out + nt((right - high.astype(F32)).astype(BF), inverse)
    return out


def eye(n):
    return (lax.broadcasted_iota(jnp.int32, (n, n), 0) == lax.broadcasted_iota(jnp.int32, (n, n), 1)).astype(BF)


def lanes_below(n):
    return (lax.broadcasted_iota(jnp.int32, (1, B), 1) < n).astype(F32)


def rows_below(n):
    return (lax.broadcasted_iota(jnp.int32, (B, 1), 0) < n).astype(F32)


def kernel(
    rhs_h, lb_h, ub_h, lp, up, ld_h, ud_h, sizes, rr_h, rl_h, ru_h, rls_h, rus_h, rld_h, rud_h, rsizes,
    out_h, outr_h,
    rhs, y0t, r1t, ych, lb, ust, ua, dl, du, rla, rua, rrin, rrt, rr, rlin, ruin, wr, dlr, dur, pbuf, xr1,
    cs, cr, gg, xa, xg, xr, sr, vg, og, lsem, ssem, rsem, csem,
):
    i = lax.axis_index("prow")
    p = lax.axis_index("pcol")
    s = lax.axis_index("layer")
    z = lax.div(i, 4)
    y = lax.rem(i, 4)

    def dev(dz=0, dy=0, dc=0, dx=0):
        return (lax.rem(z + dz, 4) * 4 + lax.rem(y + dy, 4), lax.rem(p + dx, 4), lax.rem(s + dc, 2))

    def remote(src, dst, to, send, receive=None):
        return pltpu.make_async_remote_copy(
            src_ref=src,
            dst_ref=dst,
            send_sem=ssem.at[send],
            recv_sem=rsem.at[send if receive is None else receive],
            device_id=to,
            device_id_type=MESH,
        )

    loads = {}

    def load(name, src, dst):
        copy = pltpu.make_async_copy(src, dst, lsem.at[len(loads)])
        loads[name] = copy
        copy.start()

    load("r0", rhs_h.at[0, 0, 0], rhs.at[0])
    load("d0", ld_h.at[0, 0, 0], dl.at[0])
    load("rl", rl_h.at[0], rlin)
    load("ru", ru_h.at[0], ruin)
    load("rr", rr_h.at[0], rrin)
    load("ub", ub_h.at[0, 0, 0], ust)
    load("lb", lb_h.at[0, 0, 0], lb)
    load("r1", rhs_h.at[0, 1, 0], rhs.at[1])
    load("d1", ld_h.at[0, 1, 0], dl.at[1])
    load("rls", rls_h.at[0, 0, 0], rla.at[p])
    load("rus", rus_h.at[0, 0, 0], rua.at[p])
    load("dlr", rld_h, dlr)
    load("dur", rud_h, dur)
    load("du", ud_h.at[0, :, 0], du)

    barrier = pltpu.get_barrier_semaphore()
    line = [dev(dz=d) for d in FAR] + [dev(dy=d) for d in FAR] + [dev(dx=d) for d in FAR] + [dev(dc=1)]
    for to in line:
        pl.semaphore_signal(barrier, inc=1, device_id=to, device_id_type=MESH)

    loads["r0"].wait()
    loads["d0"].wait()
    mask0 = lanes_below(sizes[0])
    mask1 = lanes_below(sizes[1])
    y0 = solve(rhs[0].T, dl[0], True) * mask0
    y0t[...] = y0
    pl.semaphore_wait(barrier, len(line))

    sends = []

    def chunk(c):
        return ych.at[y, pl.ds(W * c, W)]

    def spread_z(c):
        return [remote(chunk(c), chunk(c), dev(dz=d), S_A + 3 * c + n, S_A + c) for n, d in enumerate((1, 3, 2))]

    def spread_y(c):
        return [remote(chunk(c), chunk(c), dev(dy=d), S_B + 3 * c + n) for n, d in enumerate((2, 1, 3))]

    @pl.when(z == p)
    def _():
        ych[y] = y0.astype(BF)
        for c in range(4):
            for copy in spread_z(c):
                copy.start()
            for copy in spread_y(c):
                copy.start()

    def spread_x(src, dst, first, later=True):
        copies = [remote(src(d), dst(d), dev(dx=d), first + d) for d in FAR]
        for copy in copies:
            copy.start()
        if later:
            sends.extend(copies)
        return copies

    c_rl = spread_x(lambda d: rls_h.at[0, 0, 0], lambda d: rla.at[p], S_RL)

    loads["rl"].wait()
    loads["ru"].wait()
    mine16 = pl.ds(pl.multiple_of(16 * i, 16), 16)
    for m in range(3):
        wr[p, m, mine16, :] = jnp.where(m < p, rlin[m], ruin[m + 1])
    c_rx = spread_x(lambda d: wr.at[p, :, mine16, :], lambda d: wr.at[p, :, mine16, :], S_RX, False)

    loads["rr"].wait()
    rrt[...] = rrin[...].T.astype(BF).reshape(4, W, B)
    rr[p] = rrt[p]
    c_rr = spread_x(lambda d: rrt.at[lax.rem(p + d, 4)], lambda d: rr.at[p], S_RR)

    c_ru = spread_x(lambda d: rus_h.at[0, 0, 0], lambda d: rua.at[p], S_RU)

    loads["ub"].wait()
    for k in range(4):
        ua[4 * p + k] = ust[k] * up[0, 0, 0, k].astype(F32).astype(BF)
    mine4 = pl.ds(4 * p, 4)
    c_u = spread_x(lambda d: ua.at[mine4], lambda d: ua.at[mine4], S_U)

    @pl.when(z != p)
    def _():
        for c in range(4):
            spread_z(c)[0].wait_recv()
            for copy in spread_y(c):
                copy.start()

    loads["r1"].wait()
    loads["d1"].wait()
    loads["lb"].wait()
    r1t[...] = rhs[1].T

    for c in range(4):
        for copy in spread_y(c):
            copy.wait_recv()
    c_p = []
    own = None
    for d in (2, 1, 3, 0):
        rows = pl.ds(pl.multiple_of(W * lax.rem(p + d, 4), W), W)
        total = jnp.zeros((W, B), F32)
        for k in range(4):
            total = total + nt(ych[k, rows, :], lb[k]) * lp[0, 0, 0, k].astype(F32)
        if d == 0:
            own = total
        else:
            pbuf[d] = total.astype(BF)
            copy = remote(pbuf.at[d], xr1.at[d], dev(dx=d), S_P + d)
            copy.start()
            c_p.append(copy)
    sends.extend(c_p)

    for copy in c_rx:
        copy.wait()

    pl.semaphore_signal(csem, inc=1, device_id=dev(dc=1), device_id_type=MESH)
    half = pl.ds(2 * s, 2)
    c_rp = [remote(wr.at[half, :, mine16, :], wr.at[half, :, mine16, :], dev(*o), S_RP + n) for n, o in enumerate(SAME)]
    for copy in c_rp:
        copy.start()
    sends.extend(c_rp)

    mine = pl.ds(pl.multiple_of(W * p, W), W)
    total = own
    for copy in c_p:
        copy.wait_recv()
    for d in (1, 2, 3):
        total = total + xr1[d].astype(F32)
    y1 = solve(r1t[mine, :] - total, dl[1], True) * mask1
    y1b = y1.astype(BF)

    loads["rls"].wait()
    for copy in c_rl:
        copy.wait_recv()
    for a in range(4):
        part = nt(y1b, rla[a]).astype(BF)
        for g in range(4):
            for h in range(2):
                cs[8 * g + 2 * a + h] = part[16 * g : 16 * g + 16, 128 * h : 128 * h + 128]
    pl.semaphore_wait(csem, 1)

    def tile(o=(0, 0, 0)):
        return lax.rem(s + o[2], 2) * 16 + lax.rem(z + o[0], 4) * 4 + lax.rem(y + o[1], 4)

    my_tile = tile()
    c_rs = [remote(cs.at[tile(o)], cr.at[n], dev(*o), S_RS + n) for n, o in enumerate(PLANE)]
    for copy in c_rs:
        copy.start()
    sends.extend(c_rs)

    for copy in c_rp:
        copy.wait_recv()
    c_rc = remote(wr.at[half], wr.at[half], dev(dc=1), S_RC)
    c_rc.start()
    sends.append(c_rc)

    acc = cs[my_tile].astype(F32)
    for copy in c_rs:
        copy.wait_recv()
    for n in range(len(PLANE)):
        acc = acc + cr[n].astype(F32)
    gg[my_tile] = acc.astype(BF)
    c_ag = [remote(gg.at[my_tile], gg.at[my_tile], dev(*o), S_AG + n) for n, o in enumerate(PLANE)]
    for copy in c_ag:
        copy.start()
    sends.extend(c_ag)

    loads["dlr"].wait()
    loads["dur"].wait()
    loads["rus"].wait()
    loads["du"].wait()
    c_rc.wait_recv()
    for copy in c_rr + c_ru:
        copy.wait_recv()
    for copy in c_ag:
        copy.wait_recv()

    ys = []
    yb = []
    masks = [lanes_below(rsizes[a]) for a in range(4)]
    for a in range(4):
        coupled = jnp.concatenate(
            [
                jnp.concatenate([gg[8 * g + 2 * a + h].astype(F32) for h in range(2)], axis=1)
                for g in range(4)
            ],
            axis=0,
        )
        right = rr[a].astype(F32) - coupled
        for c in range(a):
            right = right - nn(yb[c], wr[a, c])
        ys.append(solve(right, dlr[a], True) * masks[a])
        yb.append(ys[a].astype(BF))
    xb = [None] * 4
    for a in (3, 2, 1, 0):
        right = ys[a]
        for c in range(a + 1, 4):
            right = right - nn(xb[c], wr[a, c - 1])
        xb[a] = (solve(right, dur[a], True) * masks[a]).astype(BF)
    for a in range(4):
        xr[a] = xb[a]

    right = y1
    for a in range(4):
        right = right - nt(xb[a], rua[a])
    x1b = (solve(right, du[1], True) * mask1).astype(BF)
    xa[i] = x1b
    xg[p] = x1b
    c_x = [remote(xa.at[i], xa.at[i], dev(*o), S_X + n) for n, o in enumerate(SAME)]
    for copy in c_x:
        copy.start()
    sends.extend(c_x)
    c_xg = spread_x(lambda d: xg.at[p], lambda d: xg.at[p], S_XG)
    sr[p] = xr[p]
    c_sr = spread_x(lambda d: xr.at[lax.rem(p + d, 4)], lambda d: sr.at[p], S_SR)

    for copy in c_u:
        copy.wait_recv()
    right = y0t[mine, :] - nt(xa[i], ua[i])
    for n, o in reversed(list(enumerate(SAME))):
        c_x[n].wait_recv()
        j = lax.rem(z + 4 - o[0], 4) * 4 + lax.rem(y + 4 - o[1], 4)
        right = right - nt(xa[j], ua[j])
    vg[p] = right.astype(BF)
    c_v = spread_x(lambda d: vg.at[p], lambda d: vg.at[p], S_V)

    whole = eye(B)
    for copy in c_xg:
        copy.wait_recv()
    og[1] = nt(whole, xg[...].reshape(B, B))
    o1 = pltpu.make_async_copy(og.at[1], out_h.at[0, 1, 0], lsem.at[14])
    o1.start()
    for copy in c_sr:
        copy.wait_recv()
    og[2] = nt(whole, sr[...].reshape(B, B))
    o2 = pltpu.make_async_copy(og.at[2], outr_h.at[0], lsem.at[15])
    o2.start()
    for copy in c_v:
        copy.wait_recv()
    og[0] = nt(du[0], vg[...].reshape(B, B)) * rows_below(sizes[0])
    o0 = pltpu.make_async_copy(og.at[0], out_h.at[0, 0, 0], lsem.at[16])
    o0.start()

    @pl.when(z == p)
    def _():
        for c in range(4):
            for copy in spread_z(c):
                copy.wait_send()

    for c in range(4):
        for copy in spread_y(c):
            copy.wait_send()
    for copy in sends:
        copy.wait_send()
    o1.wait()
    o2.wait()
    o0.wait()


def local(*args):
    args = list(args)
    args[7] = args[7].reshape(2)
    for n in (9, 10):
        args[n] = jnp.swapaxes(args[n], 2, 3)
    anywhere = pl.BlockSpec(memory_space=pl.ANY)
    scalars = pl.BlockSpec(memory_space=pltpu.SMEM)
    in_specs = [scalars if a.dtype == jnp.int32 else anywhere for a in args]
    v = pltpu.VMEM
    return pl.pallas_call(
        kernel,
        out_shape=(
            jax.ShapeDtypeStruct((1, 2, 1, B, B), F32),
            jax.ShapeDtypeStruct((1, B, B), F32),
        ),
        in_specs=in_specs,
        out_specs=(anywhere, anywhere),
        scratch_shapes=[
            v((2, B, B), F32),
            v((B, B), F32),
            v((B, B), F32),
            v((4, B, B), BF),
            v((4, B, B), BF),
            v((4, B, B), BF),
            v((16, B, B), BF),
            v((2, B, B), BF),
            v((2, B, B), BF),
            v((4, B, B), BF),
            v((4, B, B), BF),
            v((B, B), F32),
            v((4, W, B), BF),
            v((4, W, B), BF),
            v((4, 16, B), BF),
            v((4, 16, B), BF),
            v((4, 3, B, B), BF),
            v((4, B, B), BF),
            v((4, B, B), BF),
            v((4, W, B), BF),
            v((4, W, B), BF),
            v((32, 16, 128), BF),
            v((31, 16, 128), BF),
            v((32, 16, 128), BF),
            v((16, W, B), BF),
            v((4, W, B), BF),
            v((4, W, B), BF),
            v((4, W, B), BF),
            v((4, W, B), BF),
            v((3, B, B), F32),
            pltpu.SemaphoreType.DMA((17,)),
            pltpu.SemaphoreType.DMA((COUNT,)),
            pltpu.SemaphoreType.DMA((COUNT,)),
            pltpu.SemaphoreType.REGULAR,
        ],
        compiler_params=pltpu.CompilerParams(
            collective_id=0, has_side_effects=True, vmem_limit_bytes=60 * 2**20
        ),
    )(*args)


def solution(mesh):
    in_specs = (
        P("layer", None, "prow", None, None),
        P("layer", None, "prow", "pcol", None, None),
        P("layer", None, "prow", "pcol", None, None),
        P("layer", None, "prow", "pcol"),
        P("layer", None, "prow", "pcol"),
        P("layer", None, "prow", None, None),
        P("layer", None, "prow", None, None),
        P("layer", None, "prow"),
        P("pcol", None, None),
        P("pcol", None, None, "prow"),
        P("pcol", None, None, "prow"),
        P("layer", "pcol", "prow", None, None),
        P("layer", "prow", "pcol", None, None),
        P(),
        P(),
        P(),
    )
    out_specs = (P("layer", None, "prow", None, None), P("pcol", None, None))
    return jax.shard_map(local, mesh=mesh, in_specs=in_specs, out_specs=out_specs, check_vma=False)
```

time: 1410 us -> 82.1 us (0.06)
  waiting for transfers between devices: 1330 us -> 0 us
  Pallas kernels: 0 us -> 78.7 us
  matrix products: 29.1 us -> 0 us
  local copies, waits for them, and re-layouts: 19.2 us -> 2.62 us
    psum x20 -> x0, waiting for transfers between devices: 1240 us -> none  [the longest x8 693 us: chain_turn(): right_side = baseline - lax.psum(partial_term, 'prow')]
    all_gather x2 -> x0, waiting for transfers between devices: 96.4 us -> none  [level_step(): return (solved, lax.all_gather(narrow, 'prow', axis=0, tiled=True))]
    pallas_call x0 -> x1, Pallas kernels: none -> 78.7 us  [local(): pl.pallas_call(kernel, out_shape=(jax.ShapeDtypeStruct((1, 2, 1, B, B), F...]
    dot_general x24 -> x0, matrix products: 29.1 us -> none  [the longest x12 17.6 us: masked_solve(): jnp.einsum('nab,nbr->nar', inverse.astype(jnp.float32), right_side, preci...]
  transfers between devices with their start and end apart: 23 -> 0, of which waited for: 23 -> 0; matrix products, arithmetic and copies ran while one was open for 1% -> 0% of each run, Pallas kernels for 0% -> 0%
where the time goes in v1:
time: 82.1 us; the launch traced here: 82 us
  Pallas kernels  78.7 us (96%)
  local copies, waits for them, and re-layouts  2.62 us (3%)
    pallas_call x1, Pallas kernels, local(): pl.pallas_call(kernel, out_shape=(jax.ShapeDtypeStruct((1, 2, 1, B, B), F...  78.7 us
    unnamed x4, local copies, waits for them, and re-layouts  2.62 us

profile of v1, /device:TPU:0, one launch (start us, length us, event | category | flops | bytes accessed | tf_op | source)
XLA Modules:
  0.0 82.0 jit_solution(2099154212320347231)
XLA Ops:
  0.6 78.7 %shard_map.167 = (f32[1,2,1,256,256]{4,3,2,1,0:T(8,128)}, f32[1,256,256]{2,1,0:T(8,128)}) custom-call(f32[1,2,1,256,256]{4,3,2,1,0:T(8,128)} %rhs_h.1, bf16[1,1,1,4,256,256]{5,4,3,2,1,0:T(8,128)(2,1)} %lb_h.1, bf16[1,1,1,4,256,256]{5,4,3,2,1,0:T(8,128)(2,1)} %ub_h.1, s32[1,1,1,4]{3,2,1,0:T(1,128)} %lp.1, s32[1,1,1,4]{3,2,1,0:T(1,128)} %up.1, ...), custom_call_target="tpu_custom_call" | custom-call | tf_op jit(solution)/shard_map/pallas_call | solution.py:376
  79.4 0.0 copy-start
  79.4 1.9 %copy.20 = f32[1,2,1,256,256]{4,3,2,1,0:T(8,128)} copy(f32[1,2,1,256,256]{4,3,2,1,0:T(8,128)} %get-tuple-element.4) | data formatting | bytes 1048576
  81.3 0.0 copy-done
  81.3 0.7 copy.21
Async XLA Ops:
  79.4 1.9 %copy-start = (f32[1,256,256]{2,1,0:T(8,128)S(1)}, f32[1,256,256]{2,1,0:T(8,128)}, u32[]{:S(2)}) copy-start(f32[1,256,256]{2,1,0:T(8,128)} %get-tuple-element.5) | copy-start | bytes 786436

commit v2 on v1

--- a/solution.py
+++ b/solution.py
@@ -184,7 +184,6 @@
     for k in range(4):
         ua[4 * p + k] = ust[k] * up[0, 0, 0, k].astype(F32).astype(BF)
     mine4 = pl.ds(4 * p, 4)
-    c_u = spread_x(lambda d: ua.at[mine4], lambda d: ua.at[mine4], S_U)
 
     @pl.when(z != p)
     def _():
@@ -233,6 +232,7 @@
         copy.wait_recv()
     for d in (1, 2, 3):
         total = total + xr1[d].astype(F32)
+    c_u = spread_x(lambda d: ua.at[mine4], lambda d: ua.at[mine4], S_U)
     y1 = solve(r1t[mine, :] - total, dl[1], True) * mask1
     y1b = y1.astype(BF)
 

time: 82.1 us -> 62.1 us (0.76)
  Pallas kernels: 78.7 us -> 58.7 us
    pallas_call x1, Pallas kernels: 78.7 us -> 58.7 us  [local(): pl.pallas_call(kernel, out_shape=(jax.ShapeDtypeStruct((1, 2, 1, B, B), F...]
where the time goes in v2:
time: 62.1 us; the launch traced here: 62 us
  Pallas kernels  58.7 us (95%)
  local copies, waits for them, and re-layouts  2.62 us (4%)
  between operations  0.65 us (1%)
    pallas_call x1, Pallas kernels, local(): pl.pallas_call(kernel, out_shape=(jax.ShapeDtypeStruct((1, 2, 1, B, B), F...  58.7 us
    unnamed x4, local copies, waits for them, and re-layouts  2.62 us

profile of v2, /device:TPU:0, one launch (start us, length us, event | category | flops | bytes accessed | tf_op | source)
XLA Modules:
  0.0 62.0 jit_solution(16781330810745345812)
XLA Ops:
  0.6 58.7 %shard_map.167 = (f32[1,2,1,256,256]{4,3,2,1,0:T(8,128)}, f32[1,256,256]{2,1,0:T(8,128)}) custom-call(f32[1,2,1,256,256]{4,3,2,1,0:T(8,128)} %rhs_h.1, bf16[1,1,1,4,256,256]{5,4,3,2,1,0:T(8,128)(2,1)} %lb_h.1, bf16[1,1,1,4,256,256]{5,4,3,2,1,0:T(8,128)(2,1)} %ub_h.1, s32[1,1,1,4]{3,2,1,0:T(1,128)} %lp.1, s32[1,1,1,4]{3,2,1,0:T(1,128)} %up.1, ...), custom_call_target="tpu_custom_call" | custom-call | tf_op jit(solution)/shard_map/pallas_call | solution.py:376
  59.3 0.0 copy-start
  59.4 1.9 %copy.20 = f32[1,2,1,256,256]{4,3,2,1,0:T(8,128)} copy(f32[1,2,1,256,256]{4,3,2,1,0:T(8,128)} %get-tuple-element.4) | data formatting | bytes 1048576
  61.3 0.0 copy-done
  61.3 0.7 %copy.21 = f32[1,256,256]{2,1,0:T(8,128)} copy(f32[1,256,256]{2,1,0:T(8,128)S(1)} %copy-done) | data formatting | bytes 524288
Async XLA Ops:
  59.3 1.9 %copy-start = (f32[1,256,256]{2,1,0:T(8,128)S(1)}, f32[1,256,256]{2,1,0:T(8,128)}, u32[]{:S(2)}) copy-start(f32[1,256,256]{2,1,0:T(8,128)} %get-tuple-element.5) | copy-start | bytes 786436

commit v3 on v2

--- a/solution.py
+++ b/solution.py
@@ -35,6 +35,7 @@
 S_RL = take(4)
 S_RU = take(4)
 S_U = take(4)
+S_U2 = take(4)
 S_RX = take(4)
 S_RR = take(4)
 S_P = take(4)
@@ -80,7 +81,7 @@
     rhs_h, lb_h, ub_h, lp, up, ld_h, ud_h, sizes, rr_h, rl_h, ru_h, rls_h, rus_h, rld_h, rud_h, rsizes,
     out_h, outr_h,
     rhs, y0t, r1t, ych, lb, ust, ua, dl, du, rla, rua, rrin, rrt, rr, rlin, ruin, wr, dlr, dur, pbuf, xr1,
-    cs, cr, gg, xa, xg, xr, sr, vg, og, lsem, ssem, rsem, csem,
+    cs, cr, gg, xa, xg, xr, sr, vg, lsem, ssem, rsem, csem,
 ):
     i = lax.axis_index("prow")
     p = lax.axis_index("pcol")
@@ -134,12 +135,26 @@
     mask1 = lanes_below(sizes[1])
     y0 = solve(rhs[0].T, dl[0], True) * mask0
     y0t[...] = y0
+
+    loads["rl"].wait()
+    loads["ru"].wait()
+    mine16 = pl.ds(pl.multiple_of(16 * i, 16), 16)
+    for m in range(3):
+        wr[p, m, mine16, :] = jnp.where(m < p, rlin[m], ruin[m + 1])
+    loads["rr"].wait()
+    rrt[...] = rrin[...].T.astype(BF).reshape(4, W, B)
+    rr[p] = rrt[p]
     pl.semaphore_wait(barrier, len(line))
 
     sends = []
 
+    order = (2, 1, 3, 0)
+
+    def rows_of(c):
+        return pl.ds(pl.multiple_of(W * lax.rem(p + order[c], 4), W), W)
+
     def chunk(c):
-        return ych.at[y, pl.ds(W * c, W)]
+        return ych.at[y, rows_of(c)]
 
     def spread_z(c):
         return [remote(chunk(c), chunk(c), dev(dz=d), S_A + 3 * c + n, S_A + c) for n, d in enumerate((1, 3, 2))]
@@ -166,24 +181,10 @@
 
     c_rl = spread_x(lambda d: rls_h.at[0, 0, 0], lambda d: rla.at[p], S_RL)
 
-    loads["rl"].wait()
-    loads["ru"].wait()
-    mine16 = pl.ds(pl.multiple_of(16 * i, 16), 16)
-    for m in range(3):
-        wr[p, m, mine16, :] = jnp.where(m < p, rlin[m], ruin[m + 1])
     c_rx = spread_x(lambda d: wr.at[p, :, mine16, :], lambda d: wr.at[p, :, mine16, :], S_RX, False)
 
-    loads["rr"].wait()
-    rrt[...] = rrin[...].T.astype(BF).reshape(4, W, B)
-    rr[p] = rrt[p]
     c_rr = spread_x(lambda d: rrt.at[lax.rem(p + d, 4)], lambda d: rr.at[p], S_RR)
 
-    c_ru = spread_x(lambda d: rus_h.at[0, 0, 0], lambda d: rua.at[p], S_RU)
-
-    loads["ub"].wait()
-    for k in range(4):
-        ua[4 * p + k] = ust[k] * up[0, 0, 0, k].astype(F32).astype(BF)
-    mine4 = pl.ds(4 * p, 4)
 
     @pl.when(z != p)
     def _():
@@ -196,17 +197,21 @@
     loads["d1"].wait()
     loads["lb"].wait()
     r1t[...] = rhs[1].T
-
-    for c in range(4):
+    for k in range(4):
+        lb[k] = lb[k] * lp[0, 0, 0, k].astype(F32).astype(BF)
+    loads["ub"].wait()
+    for k in range(4):
+        ua[4 * p + k] = ust[k] * up[0, 0, 0, k].astype(F32).astype(BF)
+    mine4 = pl.ds(4 * p, 4)
+
+    c_p = []
+    own = None
+    for c, d in enumerate(order):
         for copy in spread_y(c):
             copy.wait_recv()
-    c_p = []
-    own = None
-    for d in (2, 1, 3, 0):
-        rows = pl.ds(pl.multiple_of(W * lax.rem(p + d, 4), W), W)
-        total = jnp.zeros((W, B), F32)
-        for k in range(4):
-            total = total + nt(ych[k, rows, :], lb[k]) * lp[0, 0, 0, k].astype(F32)
+        total = nt(ych[0, rows_of(c), :], lb[0])
+        for k in range(1, 4):
+            total = total + nt(ych[k, rows_of(c), :], lb[k])
         if d == 0:
             own = total
         else:
@@ -215,6 +220,7 @@
             copy.start()
             c_p.append(copy)
     sends.extend(c_p)
+    c_ru = spread_x(lambda d: rus_h.at[0, 0, 0], lambda d: rua.at[p], S_RU)
 
     for copy in c_rx:
         copy.wait()
@@ -232,7 +238,10 @@
         copy.wait_recv()
     for d in (1, 2, 3):
         total = total + xr1[d].astype(F32)
-    c_u = spread_x(lambda d: ua.at[mine4], lambda d: ua.at[mine4], S_U)
+    c_u = [remote(ua.at[mine4], ua.at[mine4], dev(dx=d), S_U + d) for d in (1, 3)]
+    for copy in c_u:
+        copy.start()
+    sends.extend(c_u)
     y1 = solve(r1t[mine, :] - total, dl[1], True) * mask1
     y1b = y1.astype(BF)
 
@@ -271,6 +280,15 @@
     for copy in c_ag:
         copy.start()
     sends.extend(c_ag)
+
+    for copy in c_u:
+        copy.wait_recv()
+    c_u2 = []
+    for d in (1, 3):
+        part = pl.ds(4 * lax.rem(p + 4 - d, 4) + (d - 1), 2)
+        c_u2.append(remote(ua.at[part], ua.at[part], dev(dx=d), S_U2 + d))
+        c_u2[-1].start()
+    sends.extend(c_u2)
 
     loads["dlr"].wait()
     loads["dur"].wait()
@@ -299,18 +317,16 @@
         ys.append(solve(right, dlr[a], True) * masks[a])
         yb.append(ys[a].astype(BF))
     xb = [None] * 4
+    top = y1
     for a in (3, 2, 1, 0):
         right = ys[a]
         for c in range(a + 1, 4):
             right = right - nn(xb[c], wr[a, c - 1])
         xb[a] = (solve(right, dur[a], True) * masks[a]).astype(BF)
-    for a in range(4):
         xr[a] = xb[a]
-
-    right = y1
-    for a in range(4):
-        right = right - nt(xb[a], rua[a])
-    x1b = (solve(right, du[1], True) * mask1).astype(BF)
+        top = top - nt(xb[a], rua[a])
+
+    x1b = (solve(top, du[1], True) * mask1).astype(BF)
     xa[i] = x1b
     xg[p] = x1b
     c_x = [remote(xa.at[i], xa.at[i], dev(*o), S_X + n) for n, o in enumerate(SAME)]
@@ -321,7 +337,7 @@
     sr[p] = xr[p]
     c_sr = spread_x(lambda d: xr.at[lax.rem(p + d, 4)], lambda d: sr.at[p], S_SR)
 
-    for copy in c_u:
+    for copy in c_u2:
         copy.wait_recv()
     right = y0t[mine, :] - nt(xa[i], ua[i])
     for n, o in reversed(list(enumerate(SAME))):
@@ -334,19 +350,13 @@
     whole = eye(B)
     for copy in c_xg:
         copy.wait_recv()
-    og[1] = nt(whole, xg[...].reshape(B, B))
-    o1 = pltpu.make_async_copy(og.at[1], out_h.at[0, 1, 0], lsem.at[14])
-    o1.start()
+    out_h[0, 1, 0] = nt(whole, xg[...].reshape(B, B))
     for copy in c_sr:
         copy.wait_recv()
-    og[2] = nt(whole, sr[...].reshape(B, B))
-    o2 = pltpu.make_async_copy(og.at[2], outr_h.at[0], lsem.at[15])
-    o2.start()
+    outr_h[0] = nt(whole, sr[...].reshape(B, B))
     for copy in c_v:
         copy.wait_recv()
-    og[0] = nt(du[0], vg[...].reshape(B, B)) * rows_below(sizes[0])
-    o0 = pltpu.make_async_copy(og.at[0], out_h.at[0, 0, 0], lsem.at[16])
-    o0.start()
+    out_h[0, 0, 0] = nt(du[0], vg[...].reshape(B, B)) * rows_below(sizes[0])
 
     @pl.when(z == p)
     def _():
@@ -359,9 +369,6 @@
             copy.wait_send()
     for copy in sends:
         copy.wait_send()
-    o1.wait()
-    o2.wait()
-    o0.wait()
 
 
 def local(*args):
@@ -369,7 +376,8 @@
     args[7] = args[7].reshape(2)
     for n in (9, 10):
         args[n] = jnp.swapaxes(args[n], 2, 3)
-    anywhere = pl.BlockSpec(memory_space=pl.ANY)
+    anywhere = pl.BlockSpec(memory_space=pltpu.HBM)
+    close = pl.BlockSpec(memory_space=pltpu.VMEM)
     scalars = pl.BlockSpec(memory_space=pltpu.SMEM)
     in_specs = [scalars if a.dtype == jnp.int32 else anywhere for a in args]
     v = pltpu.VMEM
@@ -380,7 +388,7 @@
             jax.ShapeDtypeStruct((1, B, B), F32),
         ),
         in_specs=in_specs,
-        out_specs=(anywhere, anywhere),
+        out_specs=(close, close),
         scratch_shapes=[
             v((2, B, B), F32),
             v((B, B), F32),
@@ -411,8 +419,7 @@
             v((4, W, B), BF),
             v((4, W, B), BF),
             v((4, W, B), BF),
-            v((3, B, B), F32),
-            pltpu.SemaphoreType.DMA((17,)),
+            pltpu.SemaphoreType.DMA((14,)),
             pltpu.SemaphoreType.DMA((COUNT,)),
             pltpu.SemaphoreType.DMA((COUNT,)),
             pltpu.SemaphoreType.REGULAR,

time: 62.1 us -> 61.3 us (0.987)
  Pallas kernels: 58.7 us -> 57.9 us
    pallas_call x1, Pallas kernels: 58.7 us -> 57.9 us  [local(): pl.pallas_call(kernel, out_shape=(jax.ShapeDtypeStruct((1, 2, 1, B, B), F...]
where the time goes in v3:
time: 61.3 us; the launch traced here: 61.1 us
  Pallas kernels  57.9 us (94%)
  local copies, waits for them, and re-layouts  2.62 us (4%)
  between operations  0.65 us (1%)
    pallas_call x1, Pallas kernels, local(): pl.pallas_call(kernel, out_shape=(jax.ShapeDtypeStruct((1, 2, 1, B, B), F...  57.9 us
    unnamed x4, local copies, waits for them, and re-layouts  2.62 us

profile of v3, /device:TPU:0, one launch (start us, length us, event | category | flops | bytes accessed | tf_op | source)
XLA Modules:
  0.0 61.1 jit_solution(11314228925357074061)
XLA Ops:
  0.6 57.9 %shard_map.167 = (f32[1,2,1,256,256]{4,3,2,1,0:T(8,128)}, f32[1,256,256]{2,1,0:T(8,128)}) custom-call(f32[1,2,1,256,256]{4,3,2,1,0:T(8,128)} %rhs_h.1, bf16[1,1,1,4,256,256]{5,4,3,2,1,0:T(8,128)(2,1)} %lb_h.1, bf16[1,1,1,4,256,256]{5,4,3,2,1,0:T(8,128)(2,1)} %ub_h.1, s32[1,1,1,4]{3,2,1,0:T(1,128)} %lp.1, s32[1,1,1,4]{3,2,1,0:T(1,128)} %up.1, ...), custom_call_target="tpu_custom_call" | custom-call | tf_op jit(solution)/shard_map/pallas_call | solution.py:384
  58.5 0.0 copy-start
  58.5 1.9 %copy.20 = f32[1,2,1,256,256]{4,3,2,1,0:T(8,128)} copy(f32[1,2,1,256,256]{4,3,2,1,0:T(8,128)} %get-tuple-element.4) | data formatting | bytes 1048576
  60.4 0.0 copy-done
  60.4 0.7 %copy.21 = f32[1,256,256]{2,1,0:T(8,128)} copy(f32[1,256,256]{2,1,0:T(8,128)S(1)} %copy-done) | data formatting | bytes 524288
Async XLA Ops:
  58.5 1.9 %copy-start = (f32[1,256,256]{2,1,0:T(8,128)S(1)}, f32[1,256,256]{2,1,0:T(8,128)}, u32[]{:S(2)}) copy-start(f32[1,256,256]{2,1,0:T(8,128)} %get-tuple-element.5) | copy-start | bytes 786436

commit v4 on v3

--- a/solution.py
+++ b/solution.py
@@ -136,6 +136,41 @@
     y0 = solve(rhs[0].T, dl[0], True) * mask0
     y0t[...] = y0
 
+    pl.semaphore_wait(barrier, len(line))
+
+    sends = []
+
+    order = (2, 1, 3, 0)
+
+    def rows_of(c):
+        return pl.ds(pl.multiple_of(W * lax.rem(p + order[c], 4), W), W)
+
+    def chunk(c):
+        return ych.at[y, rows_of(c)]
+
+    def spread_z(c):
+        return [remote(chunk(c), chunk(c), dev(dz=d), S_A + 3 * c + n, S_A + c) for n, d in enumerate((1, 3, 2))]
+
+    def spread_y(c):
+        return [remote(chunk(c), chunk(c), dev(dy=d), S_B + 3 * c + n) for n, d in enumerate((2, 1, 3))]
+
+    @pl.when(z == p)
+    def _():
+        ych[y] = y0.astype(BF)
+        for c in range(4):
+            for copy in spread_z(c):
+                copy.start()
+            for copy in spread_y(c):
+                copy.start()
+
+    def spread_x(src, dst, first, later=True):
+        copies = [remote(src(d), dst(d), dev(dx=d), first + d) for d in FAR]
+        for copy in copies:
+            copy.start()
+        if later:
+            sends.extend(copies)
+        return copies
+
     loads["rl"].wait()
     loads["ru"].wait()
     mine16 = pl.ds(pl.multiple_of(16 * i, 16), 16)
@@ -144,41 +179,6 @@
     loads["rr"].wait()
     rrt[...] = rrin[...].T.astype(BF).reshape(4, W, B)
     rr[p] = rrt[p]
-    pl.semaphore_wait(barrier, len(line))
-
-    sends = []
-
-    order = (2, 1, 3, 0)
-
-    def rows_of(c):
-        return pl.ds(pl.multiple_of(W * lax.rem(p + order[c], 4), W), W)
-
-    def chunk(c):
-        return ych.at[y, rows_of(c)]
-
-    def spread_z(c):
-        return [remote(chunk(c), chunk(c), dev(dz=d), S_A + 3 * c + n, S_A + c) for n, d in enumerate((1, 3, 2))]
-
-    def spread_y(c):
-        return [remote(chunk(c), chunk(c), dev(dy=d), S_B + 3 * c + n) for n, d in enumerate((2, 1, 3))]
-
-    @pl.when(z == p)
-    def _():
-        ych[y] = y0.astype(BF)
-        for c in range(4):
-            for copy in spread_z(c):
-                copy.start()
-            for copy in spread_y(c):
-                copy.start()
-
-    def spread_x(src, dst, first, later=True):
-        copies = [remote(src(d), dst(d), dev(dx=d), first + d) for d in FAR]
-        for copy in copies:
-            copy.start()
-        if later:
-            sends.extend(copies)
-        return copies
-
     c_rl = spread_x(lambda d: rls_h.at[0, 0, 0], lambda d: rla.at[p], S_RL)
 
     c_rx = spread_x(lambda d: wr.at[p, :, mine16, :], lambda d: wr.at[p, :, mine16, :], S_RX, False)
@@ -242,7 +242,7 @@
     for copy in c_u:
         copy.start()
     sends.extend(c_u)
-    y1 = solve(r1t[mine, :] - total, dl[1], True) * mask1
+    y1 = solve(r1t[mine, :] - total, dl[1], False) * mask1
     y1b = y1.astype(BF)
 
     loads["rls"].wait()
@@ -281,6 +281,16 @@
         copy.start()
     sends.extend(c_ag)
 
+    loads["dlr"].wait()
+    loads["dur"].wait()
+    loads["rus"].wait()
+    loads["du"].wait()
+    c_rc.wait_recv()
+    for copy in c_rr + c_ru:
+        copy.wait_recv()
+    for copy in c_ag:
+        copy.wait_recv()
+
     for copy in c_u:
         copy.wait_recv()
     c_u2 = []
@@ -289,16 +299,6 @@
         c_u2.append(remote(ua.at[part], ua.at[part], dev(dx=d), S_U2 + d))
         c_u2[-1].start()
     sends.extend(c_u2)
-
-    loads["dlr"].wait()
-    loads["dur"].wait()
-    loads["rus"].wait()
-    loads["du"].wait()
-    c_rc.wait_recv()
-    for copy in c_rr + c_ru:
-        copy.wait_recv()
-    for copy in c_ag:
-        copy.wait_recv()
 
     ys = []
     yb = []
@@ -314,7 +314,7 @@
         right = rr[a].astype(F32) - coupled
         for c in range(a):
             right = right - nn(yb[c], wr[a, c])
-        ys.append(solve(right, dlr[a], True) * masks[a])
+        ys.append(solve(right, dlr[a], False) * masks[a])
         yb.append(ys[a].astype(BF))
     xb = [None] * 4
     top = y1
@@ -322,11 +322,11 @@
         right = ys[a]
         for c in range(a + 1, 4):
             right = right - nn(xb[c], wr[a, c - 1])
-        xb[a] = (solve(right, dur[a], True) * masks[a]).astype(BF)
+        xb[a] = (solve(right, dur[a], False) * masks[a]).astype(BF)
         xr[a] = xb[a]
         top = top - nt(xb[a], rua[a])
 
-    x1b = (solve(top, du[1], True) * mask1).astype(BF)
+    x1b = (solve(top, du[1], False) * mask1).astype(BF)
     xa[i] = x1b
     xg[p] = x1b
     c_x = [remote(xa.at[i], xa.at[i], dev(*o), S_X + n) for n, o in enumerate(SAME)]
@@ -376,6 +376,7 @@
     args[7] = args[7].reshape(2)
     for n in (9, 10):
         args[n] = jnp.swapaxes(args[n], 2, 3)
+    args = [pltpu.with_memory_space_constraint(a, pltpu.HBM) for a in args]
     anywhere = pl.BlockSpec(memory_space=pltpu.HBM)
     close = pl.BlockSpec(memory_space=pltpu.VMEM)
     scalars = pl.BlockSpec(memory_space=pltpu.SMEM)
@@ -425,7 +426,7 @@
             pltpu.SemaphoreType.REGULAR,
         ],
         compiler_params=pltpu.CompilerParams(
-            collective_id=0, has_side_effects=True, vmem_limit_bytes=60 * 2**20
+            collective_id=0, has_side_effects=True, vmem_limit_bytes=32 * 2**20
         ),
     )(*args)
 

time: 61.3 us -> 58.3 us (0.951)
  Pallas kernels: 57.9 us -> 56 us
  local copies, waits for them, and re-layouts: 2.62 us -> 1.5 us
    pallas_call x1, Pallas kernels: 57.9 us -> 56 us  [local(): pl.pallas_call(kernel, out_shape=(jax.ShapeDtypeStruct((1, 2, 1, B, B), F...]
    unnamed x4 -> x2, local copies, waits for them, and re-layouts: 2.62 us -> 1.5 us
where the time goes in v4:
time: 58.3 us; the launch traced here: 58.2 us
  Pallas kernels  56 us (96%)
  local copies, waits for them, and re-layouts  1.5 us (3%)
  between operations  0.65 us (1%)
    pallas_call x1, Pallas kernels, local(): pl.pallas_call(kernel, out_shape=(jax.ShapeDtypeStruct((1, 2, 1, B, B), F...  56 us
    unnamed x2, local copies, waits for them, and re-layouts  1.5 us

profile of v4, /device:TPU:0, one launch (start us, length us, event | category | flops | bytes accessed | tf_op | source)
XLA Modules:
  0.0 58.2 jit_solution(13656920770967263677)
XLA Ops:
  0.6 56.0 %shard_map.167 = (f32[1,2,1,256,256]{4,3,2,1,0:T(8,128)S(1)}, f32[1,256,256]{2,1,0:T(8,128)S(1)}) custom-call(f32[1,2,1,256,256]{4,3,2,1,0:T(8,128)} %rhs_h.1, bf16[1,1,1,4,256,256]{5,4,3,2,1,0:T(8,128)(2,1)} %lb_h.1, bf16[1,1,1,4,256,256]{5,4,3,2,1,0:T(8,128)(2,1)} %ub_h.1, s32[1,1,1,4]{3,2,1,0:T(1,128)} %lp.1, s32[1,1,1,4]{3,2,1,0:T(1,128)} %up.1, ...), custom_call_target="tpu_custom_call" | custom-call | tf_op jit(solution)/shard_map/pallas_call | solution.py:385
  56.7 0.8 %copy.20 = f32[1,2,1,256,256]{4,3,2,1,0:T(8,128)} copy(f32[1,2,1,256,256]{4,3,2,1,0:T(8,128)S(1)} %get-tuple-element.4) | data formatting | bytes 1048576
  57.5 0.7 %copy.21 = f32[1,256,256]{2,1,0:T(8,128)} copy(f32[1,256,256]{2,1,0:T(8,128)S(1)} %get-tuple-element.5) | data formatting | bytes 524288

commit v5 on v4

--- a/solution.py
+++ b/solution.py
@@ -227,10 +227,6 @@
 
     pl.semaphore_signal(csem, inc=1, device_id=dev(dc=1), device_id_type=MESH)
     half = pl.ds(2 * s, 2)
-    c_rp = [remote(wr.at[half, :, mine16, :], wr.at[half, :, mine16, :], dev(*o), S_RP + n) for n, o in enumerate(SAME)]
-    for copy in c_rp:
-        copy.start()
-    sends.extend(c_rp)
 
     mine = pl.ds(pl.multiple_of(W * p, W), W)
     total = own
@@ -242,7 +238,7 @@
     for copy in c_u:
         copy.start()
     sends.extend(c_u)
-    y1 = solve(r1t[mine, :] - total, dl[1], False) * mask1
+    y1 = solve(r1t[mine, :] - total, dl[1], True) * mask1
     y1b = y1.astype(BF)
 
     loads["rls"].wait()
@@ -263,12 +259,11 @@
     for copy in c_rs:
         copy.start()
     sends.extend(c_rs)
-
+    c_rp = [remote(wr.at[half, :, mine16, :], wr.at[half, :, mine16, :], dev(*o), S_RP + n) for n, o in enumerate(SAME)]
     for copy in c_rp:
-        copy.wait_recv()
-    c_rc = remote(wr.at[half], wr.at[half], dev(dc=1), S_RC)
-    c_rc.start()
-    sends.append(c_rc)
+        copy.start()
+    sends.extend(c_rp)
+
 
     acc = cs[my_tile].astype(F32)
     for copy in c_rs:
@@ -280,6 +275,11 @@
     for copy in c_ag:
         copy.start()
     sends.extend(c_ag)
+    for copy in c_rp:
+        copy.wait_recv()
+    c_rc = remote(wr.at[half], wr.at[half], dev(dc=1), S_RC)
+    c_rc.start()
+    sends.append(c_rc)
 
     loads["dlr"].wait()
     loads["dur"].wait()
@@ -314,7 +314,7 @@
         right = rr[a].astype(F32) - coupled
         for c in range(a):
             right = right - nn(yb[c], wr[a, c])
-        ys.append(solve(right, dlr[a], False) * masks[a])
+        ys.append(solve(right, dlr[a], True) * masks[a])
         yb.append(ys[a].astype(BF))
     xb = [None] * 4
     top = y1
@@ -326,11 +326,11 @@
         xr[a] = xb[a]
         top = top - nt(xb[a], rua[a])
 
-    x1b = (solve(top, du[1], False) * mask1).astype(BF)
+    x1b = (solve(top, du[1], True) * mask1).astype(BF)
     xa[i] = x1b
     xg[p] = x1b
     c_x = [remote(xa.at[i], xa.at[i], dev(*o), S_X + n) for n, o in enumerate(SAME)]
-    for copy in c_x:
+    for copy in reversed(c_x):
         copy.start()
     sends.extend(c_x)
     c_xg = spread_x(lambda d: xg.at[p], lambda d: xg.at[p], S_XG)

time: 58.3 us -> 57.7 us (0.990)
  Pallas kernels: 56 us -> 55.4 us
    pallas_call x1, Pallas kernels: 56 us -> 55.4 us  [local(): pl.pallas_call(kernel, out_shape=(jax.ShapeDtypeStruct((1, 2, 1, B, B), F...]
where the time goes in v5:
time: 57.7 us; the launch traced here: 57.5 us
  Pallas kernels  55.4 us (96%)
  local copies, waits for them, and re-layouts  1.5 us (3%)
  between operations  0.65 us (1%)
    pallas_call x1, Pallas kernels, local(): pl.pallas_call(kernel, out_shape=(jax.ShapeDtypeStruct((1, 2, 1, B, B), F...  55.4 us
    unnamed x2, local copies, waits for them, and re-layouts  1.5 us

profile of v5, /device:TPU:0, one launch (start us, length us, event | category | flops | bytes accessed | tf_op | source)
XLA Modules:
  0.0 57.5 jit_solution(15343585382746403499)
XLA Ops:
  0.6 55.4 %shard_map.167 = (f32[1,2,1,256,256]{4,3,2,1,0:T(8,128)S(1)}, f32[1,256,256]{2,1,0:T(8,128)S(1)}) custom-call(f32[1,2,1,256,256]{4,3,2,1,0:T(8,128)} %rhs_h.1, bf16[1,1,1,4,256,256]{5,4,3,2,1,0:T(8,128)(2,1)} %lb_h.1, bf16[1,1,1,4,256,256]{5,4,3,2,1,0:T(8,128)(2,1)} %ub_h.1, s32[1,1,1,4]{3,2,1,0:T(1,128)} %lp.1, s32[1,1,1,4]{3,2,1,0:T(1,128)} %up.1, ...), custom_call_target="tpu_custom_call" | custom-call | tf_op jit(solution)/shard_map/pallas_call | solution.py:385
  56.0 0.8 %copy.20 = f32[1,2,1,256,256]{4,3,2,1,0:T(8,128)} copy(f32[1,2,1,256,256]{4,3,2,1,0:T(8,128)S(1)} %get-tuple-element.4) | data formatting | bytes 1048576
  56.8 0.7 %copy.21 = f32[1,256,256]{2,1,0:T(8,128)} copy(f32[1,256,256]{2,1,0:T(8,128)S(1)} %get-tuple-element.5) | data formatting | bytes 524288

commit v6 on v5

--- a/solution.py
+++ b/solution.py
@@ -234,10 +234,6 @@
         copy.wait_recv()
     for d in (1, 2, 3):
         total = total + xr1[d].astype(F32)
-    c_u = [remote(ua.at[mine4], ua.at[mine4], dev(dx=d), S_U + d) for d in (1, 3)]
-    for copy in c_u:
-        copy.start()
-    sends.extend(c_u)
     y1 = solve(r1t[mine, :] - total, dl[1], True) * mask1
     y1b = y1.astype(BF)
 
@@ -259,6 +255,10 @@
     for copy in c_rs:
         copy.start()
     sends.extend(c_rs)
+    c_u = [remote(ua.at[mine4], ua.at[mine4], dev(dx=d), S_U + d) for d in (1, 3)]
+    for copy in c_u:
+        copy.start()
+    sends.extend(c_u)
     c_rp = [remote(wr.at[half, :, mine16, :], wr.at[half, :, mine16, :], dev(*o), S_RP + n) for n, o in enumerate(SAME)]
     for copy in c_rp:
         copy.start()
@@ -353,7 +353,7 @@
     out_h[0, 1, 0] = nt(whole, xg[...].reshape(B, B))
     for copy in c_sr:
         copy.wait_recv()
-    outr_h[0] = nt(whole, sr[...].reshape(B, B))
+    outr_h[0] = nt(whole, sr[...].reshape(B, B)).astype(BF)
     for copy in c_v:
         copy.wait_recv()
     out_h[0, 0, 0] = nt(du[0], vg[...].reshape(B, B)) * rows_below(sizes[0])
@@ -382,11 +382,11 @@
     scalars = pl.BlockSpec(memory_space=pltpu.SMEM)
     in_specs = [scalars if a.dtype == jnp.int32 else anywhere for a in args]
     v = pltpu.VMEM
-    return pl.pallas_call(
+    sub, root = pl.pallas_call(
         kernel,
         out_shape=(
             jax.ShapeDtypeStruct((1, 2, 1, B, B), F32),
-            jax.ShapeDtypeStruct((1, B, B), F32),
+            jax.ShapeDtypeStruct((1, B, B), BF),
         ),
         in_specs=in_specs,
         out_specs=(close, close),
@@ -429,6 +429,7 @@
             collective_id=0, has_side_effects=True, vmem_limit_bytes=32 * 2**20
         ),
     )(*args)
+    return sub, root.astype(F32)
 
 
 def solution(mesh):

time: 57.7 us -> 57.7 us (level)
  other arithmetic: 0 us -> 0.72 us
  local copies, waits for them, and re-layouts: 1.5 us -> 0.79 us
    convert_element_type x0 -> x1, other arithmetic: none -> 0.72 us  [local(): return (sub, root.astype(F32))]
    unnamed x2 -> x1, local copies, waits for them, and re-layouts: 1.5 us -> 0.79 us
where the time goes in v6:
time: 57.7 us; the launch traced here: 57.6 us
  Pallas kernels  55.4 us (96%)
  local copies, waits for them, and re-layouts  0.79 us (1%)
  other arithmetic  0.72 us (1%)
  between operations  0.65 us (1%)
    pallas_call x1, Pallas kernels, local(): pl.pallas_call(kernel, out_shape=(jax.ShapeDtypeStruct((1, 2, 1, B, B), F...  55.4 us

profile of v6, /device:TPU:0, one launch (start us, length us, event | category | flops | bytes accessed | tf_op | source)
XLA Modules:
  0.0 57.6 jit_solution(10169451167199493308)
XLA Ops:
  0.6 55.4 %shard_map.167 = (f32[1,2,1,256,256]{4,3,2,1,0:T(8,128)S(1)}, bf16[1,256,256]{2,1,0:T(8,128)(2,1)S(1)}) custom-call(f32[1,2,1,256,256]{4,3,2,1,0:T(8,128)} %rhs_h.1, bf16[1,1,1,4,256,256]{5,4,3,2,1,0:T(8,128)(2,1)} %lb_h.1, bf16[1,1,1,4,256,256]{5,4,3,2,1,0:T(8,128)(2,1)} %ub_h.1, s32[1,1,1,4]{3,2,1,0:T(1,128)} %lp.1, s32[1,1,1,4]{3,2,1,0:T(1,128)} %up.1, ...), custom_call_target="tpu_custom_call" | custom-call | tf_op jit(solution)/shard_map/pallas_call | solution.py:385
  56.0 0.7 %convert_element_type.3 = f32[1,256,256]{2,1,0:T(8,128)} convert(bf16[1,256,256]{2,1,0:T(8,128)(2,1)S(1)} %get-tuple-element.5) | non-fusion elementwise | flops 65536 | bytes 393216 | tf_op jit(solution)/shard_map/convert_element_type | solution.py:432
  56.8 0.8 %copy.19 = f32[1,2,1,256,256]{4,3,2,1,0:T(8,128)} copy(f32[1,2,1,256,256]{4,3,2,1,0:T(8,128)S(1)} %get-tuple-element.8) | data formatting | bytes 1048576

commit v7 on v5

--- a/solution.py
+++ b/solution.py
@@ -160,6 +160,7 @@
         for c in range(4):
             for copy in spread_z(c):
                 copy.start()
+        for c in range(4):
             for copy in spread_y(c):
                 copy.start()
 

time: 57.7 us -> 57.7 us (level)
  no operation moved by 1% of the time
where the time goes in v7:
time: 57.7 us; the launch traced here: 57.5 us
  Pallas kernels  55.4 us (96%)
  local copies, waits for them, and re-layouts  1.5 us (3%)
  between operations  0.65 us (1%)
    pallas_call x1, Pallas kernels, local(): pl.pallas_call(kernel, out_shape=(jax.ShapeDtypeStruct((1, 2, 1, B, B), F...  55.4 us
    unnamed x2, local copies, waits for them, and re-layouts  1.5 us

profile of v7, /device:TPU:0, one launch (start us, length us, event | category | flops | bytes accessed | tf_op | source)
XLA Modules:
  0.0 57.5 jit_solution(7181623564365626486)
XLA Ops:
  0.6 55.4 %shard_map.167 = (f32[1,2,1,256,256]{4,3,2,1,0:T(8,128)S(1)}, f32[1,256,256]{2,1,0:T(8,128)S(1)}) custom-call(f32[1,2,1,256,256]{4,3,2,1,0:T(8,128)} %rhs_h.1, bf16[1,1,1,4,256,256]{5,4,3,2,1,0:T(8,128)(2,1)} %lb_h.1, bf16[1,1,1,4,256,256]{5,4,3,2,1,0:T(8,128)(2,1)} %ub_h.1, s32[1,1,1,4]{3,2,1,0:T(1,128)} %lp.1, s32[1,1,1,4]{3,2,1,0:T(1,128)} %up.1, ...), custom_call_target="tpu_custom_call" | custom-call | tf_op jit(solution)/shard_map/pallas_call | solution.py:386
  56.0 0.8 %copy.20 = f32[1,2,1,256,256]{4,3,2,1,0:T(8,128)} copy(f32[1,2,1,256,256]{4,3,2,1,0:T(8,128)S(1)} %get-tuple-element.4) | data formatting | bytes 1048576
  56.8 0.7 %copy.21 = f32[1,256,256]{2,1,0:T(8,128)} copy(f32[1,256,256]{2,1,0:T(8,128)S(1)} %get-tuple-element.5) | data formatting | bytes 524288
